TPU v7x, 256 devices: a whole 4x4x8 slice. The times are simulated.
256 devices in a mesh: grp: 4 (over z_hi, core), dev: 64 (over z_lo, y, x).
Axes of the slice: x: 4, y: 4, z: 8 (z_hi: 2, z_lo: 4; z = z_hi * 4 + z_lo), core: 2. Of those that a mesh axis runs over, the one named last changes fastest.
Arguments:
- key_tokens: bfloat16 [32768, 768], P(('grp', 'dev')), may hold values from -6 to 6
- value_tokens: bfloat16 [32768, 768], P(('grp', 'dev')), may hold values from -6 to 6
- queries: bfloat16 [32768, 768], P(('grp', 'dev')), may hold values from -192 to 192
- token_rate: float32 [32768], P(('grp', 'dev')), may hold values from 0.00019934 to 0.00159472
- fast_weights: bfloat16 [3, 1536, 768], P(None, ('grp', 'dev')), may hold values from -0.21875 to 0.21875
Outputs:
- target_out: bfloat16 [32768, 768], P(('grp', 'dev'))
All inputs are finite; a program needn't handle non-finite values.
Results may differ from a plain program's by a relative error of at most 0.012.
The roundings to bfloat16 on the way count: a program that leaves them out, or rounds other values in their place, can miss the bound.
Values may be sent and summed in bfloat16 or wider, within the bound.
A program may use at most 64 MiB of HBM per device.

v0:
```python
import jax
import jax.numpy as jnp
from jax import lax
from jax.sharding import PartitionSpec as P

D = 768
HEADS = 12
HEAD_DIM = 64


epsilon = 1e-06


def rms_rows(matrix):
    return matrix / jnp.sqrt(jnp.mean(matrix * matrix, axis=-1, keepdims=True) + epsilon)


def gradient_rows(weights, key_normed, signal):
    gate_act = jnp.dot(key_normed, weights[0].T, preferred_element_type=jnp.float32)
    up_act = jnp.dot(key_normed, weights[1].T, preferred_element_type=jnp.float32)
    sigmoid_gate = jax.nn.sigmoid(gate_act)
    silu_gate = gate_act * sigmoid_gate
    hidden_bf = (silu_gate * up_act).astype(jnp.bfloat16)
    down_grad = jnp.dot(hidden_bf.T, signal, preferred_element_type=jnp.float32)
    hidden_grad = jnp.dot(signal, weights[2].T, preferred_element_type=jnp.float32)
    gate_grad = (
        hidden_grad * up_act * sigmoid_gate * (1.0 + gate_act * (1.0 - sigmoid_gate))
    ).astype(jnp.bfloat16)
    up_grad = (hidden_grad * silu_gate).astype(jnp.bfloat16)
    return jnp.stack(
        [
            jnp.dot(gate_grad.T, key_normed, preferred_element_type=jnp.float32),
            jnp.dot(up_grad.T, key_normed, preferred_element_type=jnp.float32),
            down_grad,
        ]
    )


def normalize_rows(old_bf, grad_rows):
    old_rows = old_bf.astype(jnp.float32)
    stepped = old_rows - grad_rows
    return (
        stepped
        * jnp.sqrt(jnp.mean(old_rows * old_rows, axis=-1, keepdims=True) + epsilon)
        / jnp.sqrt(jnp.mean(stepped * stepped, axis=-1, keepdims=True) + epsilon)
    ).astype(jnp.bfloat16)


def local_attention(query_block, key_block, value_block):
    query_count = query_block.shape[0]
    key_count = key_block.shape[0]
    query_heads = query_block.reshape(query_count, HEADS, HEAD_DIM)
    key_heads = key_block.reshape(key_count, HEADS, HEAD_DIM)
    value_heads = value_block.reshape(key_count, HEADS, HEAD_DIM)
    scores = jnp.einsum(
        "qhe,khe->hqk", query_heads, key_heads, preferred_element_type=jnp.float32
    ) * HEAD_DIM ** (-0.5)
    weights_bf = jax.nn.softmax(scores, axis=-1).astype(jnp.bfloat16)
    mixed = jnp.einsum("hqk,khe->qhe", weights_bf, value_heads, preferred_element_type=jnp.float32)
    return mixed.reshape(query_count, D)


def body(key_tokens, value_tokens, queries, token_rate, fast_weights):
    key_normed = rms_rows(key_tokens.astype(jnp.float32)).astype(jnp.bfloat16)
    signal = (-(token_rate[:, None] * value_tokens.astype(jnp.float32))).astype(jnp.bfloat16)
    all_keys, all_signals = (
        lax.all_gather(key_normed, "grp", axis=0, tiled=True),
        lax.all_gather(signal, "grp", axis=0, tiled=True),
    )
    attention_out = local_attention(queries, key_tokens, value_tokens)
    query_normed = rms_rows(queries.astype(jnp.float32)).astype(jnp.bfloat16)
    group_grad = gradient_rows(
        lax.all_gather(fast_weights, "dev", axis=1, tiled=True), all_keys, all_signals
    )
    owned_grad = lax.psum_scatter(group_grad, "dev", scatter_dimension=1, tiled=True)
    updated = normalize_rows(fast_weights, owned_grad)
    shard_rows = lax.all_gather(updated, ("grp", "dev"), axis=1, tiled=True)
    gate_act = jnp.dot(query_normed, shard_rows[0].T, preferred_element_type=jnp.float32)
    up_act = jnp.dot(query_normed, shard_rows[1].T, preferred_element_type=jnp.float32)
    hidden_bf = (jax.nn.silu(gate_act) * up_act).astype(jnp.bfloat16)
    fast_out = jnp.dot(hidden_bf, shard_rows[2], preferred_element_type=jnp.float32)
    return (fast_out + attention_out).astype(jnp.bfloat16)


def solution(mesh):
    in_specs = (
        P(("grp", "dev"), None),
        P(("grp", "dev"), None),
        P(("grp", "dev"), None),
        P(("grp", "dev")),
        P(None, ("grp", "dev"), None),
    )
    out_specs = P(("grp", "dev"), None)
    return jax.shard_map(body, mesh=mesh, in_specs=in_specs, out_specs=out_specs, check_vma=False)
```

profile of v0, /device:TPU:1, one launch (start us, length us, event | category | flops | bytes accessed | tf_op | source)
XLA Modules:
  0.0 1850.1 jit_solution(13766219696843032451)
XLA Ops:
  6.5 0.0 all-gather.3.cloned.1.call-start
  6.5 1.4 copy.23
  7.9 0.0 all-gather.3.cloned.1.call-update
  8.0 0.0 all-reduce.3.cloned.1.call-start
  8.0 1.0 fusion.19
  9.1 1.0 fusion.20
  10.1 1.0 negate_convert_fusion
  11.2 17.2 all_gather.14
  28.4 16.0 all_gather.12
  44.4 277.1 %all-gather.3.cloned.1.call-done = bf16[3,384,768]{2,0,1:T(4,128)(2,1)} async-done(((bf16[3,6,768]{2,0,1:T(4,128)(2,1)}), bf16[3,384,768]{2,0,1:T(4,128)(2,1)}) %all-gather.3.cloned.1.call-update) | async-done | bytes 1769488 | tf_op jit(solution)/shard_map/all_gather | solution.py:73
  321.4 6.5 fusion.37
  328.0 0.6 fusion.14
  328.6 0.6 fusion.15
  329.2 0.6 fusion.16
  329.8 0.6 convolution_bitcast_fusion.1
  330.3 0.7 convolution_bitcast_fusion.2
  331.1 0.6 convolution_bitcast_fusion
  331.6 2.0 pad_maximum_fusion
  333.7 0.0 copy-start.4
  333.7 0.0 copy-start.3
  333.7 0.0 copy-start
  333.7 0.0 copy-start.1
  333.7 0.0 copy-start.2
  333.7 0.0 all-reduce.3.cloned.1.call-update
  333.7 0.0 all-gather.5.cloned.1.call-start
  333.8 0.6 copy-done.4
  334.3 0.6 dynamic-slice
  335.6 716.0 %all-reduce.3.cloned.1.call-done = f32[3,384,768]{2,1,0:T(8,128)} async-done(((f32[3,384,768]{2,1,0:T(8,128)}), f32[3,384,768]{2,1,0:T(8,128)}) %all-reduce.3.cloned.1.call-update) | async-done | bytes 3538960
  1051.6 0.0 copy-done.3
  1051.6 1.0 fusion.26
  1052.6 1.0 divide_convert_fusion.2
  1053.7 0.6 copy.27
  1054.3 0.0 all-gather.5.cloned.1.call-update
  1054.3 0.0 copy-done
  1054.3 0.2 copy.32
  1054.5 0.0 copy-done.1
  1054.5 0.2 copy.33
  1054.7 0.0 copy-done.2
  1054.7 0.2 copy.31
  1054.8 0.4 fusion.38
  1055.3 0.3 convolution_multiply_fusion.1
  1055.6 0.3 fusion.23
  1055.9 0.2 copy.35
  1056.1 0.1 fusion.17
  1056.2 760.7 %all-gather.5.cloned.1.call-done = bf16[3,1536,768]{2,0,1:T(4,128)(2,1)} async-done(((bf16[3,6,768]{2,0,1:T(4,128)(2,1)}), bf16[3,1536,768]{2,0,1:T(4,128)(2,1)}) %all-gather.5.cloned.1.call-update) | async-done | bytes 7077904 | tf_op jit(solution)/shard_map/all_gather | solution.py:77
  1817.0 19.9 %fusion.36 = (bf16[1,1536,768]{2,0,1:T(2,128)(2,1)S(1)}, bf16[1,1536,768]{2,0,1:T(2,128)(2,1)}, bf16[1,1536,768]{2,0,1:T(2,128)(2,1)}) fusion(bf16[3,1536,768]{2,0,1:T(4,128)(2,1)} %all-gather.5.cloned.1.call-done), kind=kLoop, calls=%fused_computation.61 | loop fusion | bytes 14155776 | tf_op jit(solution)/shard_map/slice | solution.py:78
  1836.8 0.9 fusion.3
  1837.8 5.8 fusion.7
  (3 shorter events, 0.0 us)
Async XLA Ops:
  6.5 314.9 %all-gather.3.cloned.1.call-start = ((), (), s32[]{:S(2)}) async-start(), calls=%async_computation | async-start | bytes 2396160 | tf_op jit(solution)/shard_map/all_gather | solution.py:73
  8.0 1043.7 %all-reduce.3.cloned.1.call-start = ((), (), s32[]{:S(2)}) async-start(), calls=%async_computation.2 | async-start | bytes 7077888
  333.7 0.7 copy-start.4
  333.7 718.0 %copy-start.3 = (bf16[3,6,768]{2,1,0:T(8,128)(2,1)S(1)}, bf16[3,6,768]{2,1,0:T(8,128)(2,1)}, u32[]{:S(2)}) copy-start(bf16[3,6,768]{2,1,0:T(8,128)(2,1)} %param.9) | copy-start | bytes 82948
  333.7 720.6 %copy-start = (bf16[128,768]{1,0:T(8,128)(2,1)S(1)}, bf16[128,768]{1,0:T(8,128)(2,1)}, u32[]{:S(2)}) copy-start(bf16[128,768]{1,0:T(8,128)(2,1)} %param.5) | copy-start | bytes 589828
  333.7 720.8 %copy-start.1 = (bf16[128,768]{1,0:T(8,128)(2,1)S(1)}, bf16[128,768]{1,0:T(8,128)(2,1)}, u32[]{:S(2)}) copy-start(bf16[128,768]{1,0:T(8,128)(2,1)} %param.6) | copy-start | bytes 589828
  333.7 721.0 %copy-start.2 = (bf16[128,768]{1,0:T(8,128)(2,1)S(1)}, bf16[128,768]{1,0:T(8,128)(2,1)}, u32[]{:S(2)}) copy-start(bf16[128,768]{1,0:T(8,128)(2,1)} %param.7) | copy-start | bytes 589828
  333.7 1483.3 %all-gather.5.cloned.1.call-start = ((), (), s32[]{:S(2)}) async-start(), calls=%async_computation.1 | async-start | bytes 9474048 | tf_op jit(solution)/shard_map/all_gather | solution.py:77
Sparse Core Ops, SparseCore 0:
  9.1 312.2 all-gather.2
  333.8 717.7 all-reduce.2
  1054.4 762.4 all-gather.4
where the time goes:
time: 1850 us
  waiting for transfers between devices  1750 us (95%)
  blocking collectives  33.2 us (2%)
  local copies, waits for them, and re-layouts  30.2 us (2%)
    all_gather x1, waiting for transfers between devices, body(): shard_rows = lax.all_gather(updated, ('grp', 'dev'), axis=1, tiled=True)  761 us
    unnamed x4, waiting for transfers between devices  716 us
    all_gather x1, waiting for transfers between devices, body(): lax.all_gather(fast_weights, 'dev', axis=1, tiled=True)  277 us
  transfers between devices with their start and end apart: 3, of which 3 were waited for; matrix products, arithmetic and copies ran while one was open for 0% of the time, Pallas kernels for 0%

commit v1 on v0

v1 whole, which is shorter than its diff:
```python
import functools

import jax
import jax.numpy as jnp
from jax import lax
from jax.experimental import pallas as pl
from jax.experimental.pallas import tpu as pltpu
from jax.sharding import PartitionSpec as P

D = 768
TOK = 128
EPS = 1e-06
NX, NY, NZ = 4, 4, 8
ROWS = 6
BLK = NZ * ROWS
PACK = 48
MESH = pl.DeviceIdType.MESH
F32 = jnp.float32
BF16 = jnp.bfloat16


def dot_nt(a, b):
    return lax.dot_general(a, b, (((1,), (1,)), ((), ())), preferred_element_type=F32)


def dot_nn(a, b):
    return lax.dot_general(a, b, (((1,), (0,)), ((), ())), preferred_element_type=F32)


def device(x, y, z, c):
    return ((z // 4) * 2 + c, (z % 4) * 16 + y * 4 + x)


def rms_scale(rows):
    return lax.rsqrt(jnp.mean(rows * rows, axis=-1, keepdims=True) + EPS)


def kernel(
    key_ref, val_ref, qry_ref, rate_ref, w_ref, out_ref,
    wpk, az0, w, ks, qn, act, rys, ryr, rzs, rzr, az1, wu, unp, gu, hid_q, fo, ps, pr, att,
    s_az0, r_az0, s_wy, r_wy, s_tok, r_tok, s_tokc, r_tokc, s_q, r_q,
    s_ry, r_ry, s_rz, r_rz, s_az, r_az, s_ay, r_ay, s_ac, r_ac, s_p, r_p,
):
    g = lax.axis_index("grp")
    d = lax.axis_index("dev")
    x, y, z, c = d % 4, (d // 4) % 4, (g // 2) * 4 + d // 16, g % 2
    other = device(x, y, z, 1 - c)
    xs = [device((x + k) % NX, y, z, c) for k in range(NX)]
    ys = [device(x, (y + k) % NY, z, c) for k in range(NY)]
    zs = [device(x, y, (z + k) % NZ, c) for k in range(NZ)]

    barrier = pltpu.get_barrier_semaphore()
    peers = [other] + xs[1:] + ys[1:] + zs[1:]
    for peer in peers:
        pl.semaphore_signal(barrier, inc=1, device_id=peer, device_id_type=MESH)
    pl.semaphore_wait(barrier, len(peers))

    def send(src, dst, ssem, rsem, peer):
        pltpu.make_async_remote_copy(
            src_ref=src, dst_ref=dst, send_sem=ssem, recv_sem=rsem, device_id=peer, device_id_type=MESH
        ).start()

    def wait(ref, sem):
        pltpu.make_async_copy(ref, ref, sem).wait()

    wpk[...] = jnp.zeros_like(wpk)
    for m in range(3):
        rows = w_ref[m].astype(F32)
        for j in range(6):
            wpk[m, j * 8 : j * 8 + ROWS, :] = rows[:, j * 128 : (j + 1) * 128]
    az0[z] = wpk[...].astype(BF16)
    for k in range(1, NZ):
        send(az0.at[z], az0.at[z], s_az0, r_az0, zs[k])

    slot = x * 2 + c
    keys = key_ref[...].astype(F32)
    ks[0, slot] = (keys * rms_scale(keys)).astype(BF16)
    ks[1, slot] = (-(rate_ref[...] * val_ref[...].astype(F32))).astype(BF16)
    for k in (2, 1, 3):
        send(ks.at[:, slot], ks.at[:, slot], s_tok.at[k - 1], r_tok.at[k - 1], xs[k])
    send(ks.at[:, slot], ks.at[:, slot], s_tokc.at[0], r_tokc.at[0], other)
    queries = qry_ref[...].astype(F32)
    qn[x] = (queries * rms_scale(queries)).astype(BF16)

    def unpack(m, piece, store):
        for zz in range(NZ):
            unp[m, :, zz * ROWS : zz * ROWS + 8, :] = piece(zz).astype(F32).reshape(6, 8, 128)
        for j in range(6):
            store(j, unp[m, j, :BLK, :].astype(BF16))

    wait(az0.at[pl.ds(0, NZ - 1)], r_az0)
    for m in range(3):
        def put_old(j, v, m=m):
            w[m, y, :, j * 128 : (j + 1) * 128] = v
        unpack(m, lambda zz, m=m: az0[zz, m], put_old)
    for k in range(1, NY):
        send(w.at[:, y], w.at[:, y], s_wy, r_wy, ys[k])

    lane = lax.broadcasted_iota(jnp.int32, (TOK, 128), 1)
    for p in range(6):
        cols = slice(p * 128, (p + 1) * 128)
        qp, kp, vp = qry_ref[:, cols], key_ref[:, cols], val_ref[:, cols]
        zero = jnp.zeros_like(qp)
        both = jnp.concatenate([jnp.where(lane < 64, qp, zero), jnp.where(lane < 64, zero, qp)], axis=0)
        scores = dot_nt(both, kp) * 0.125
        e = jnp.exp(scores - jnp.max(scores, axis=-1, keepdims=True))
        probs = (e / jnp.sum(e, axis=-1, keepdims=True)).astype(BF16)
        mixed = dot_nn(probs, vp)
        att[:, cols] = jnp.where(lane < 64, mixed[:TOK], mixed[TOK:])

    def token_slot(k, core):
        return ((x + NX - k) % NX) * 2 + core
    for k in (1, 3, 2):
        sl = token_slot(k, c)
        wait(ks.at[:, sl], r_tok.at[k - 1])
        send(ks.at[:, sl], ks.at[:, sl], s_tokc.at[k], r_tokc.at[k], other)
    for k in (2, 1, 3):
        send(qn.at[x], qn.at[x], s_q, r_q, xs[k])

    wait(w.at[:, pl.ds(0, NY - 1)], r_wy)
    w1 = w[0].reshape(NY * BLK, D)
    w3 = w[1].reshape(NY * BLK, D)
    w2 = w[2].reshape(NY * BLK, D)
    for k in (0, 1, 3, 2):
        sl = token_slot(k, 1 - c)
        wait(ks.at[:, sl], r_tokc.at[k])
        xx = (x + NX - k) % NX
        kn = ks[0, pl.ds(xx * 2, 2)].reshape(2 * TOK, D)
        sg = ks[1, pl.ds(xx * 2, 2)].reshape(2 * TOK, D)
        gate = dot_nt(w1, kn)
        up = dot_nt(w3, kn)
        hgrad = dot_nt(w2, sg)
        sig = jax.nn.sigmoid(gate)
        silu = gate * sig
        act[2, xx] = (silu * up).astype(BF16)
        act[0, xx] = (hgrad * up * sig * (1.0 + gate * (1.0 - sig))).astype(BF16)
        act[1, xx] = (hgrad * silu).astype(BF16)

    order = (2, 0, 1)
    for m in order:
        src = 1 if m == 2 else 0
        total = None
        for xx in range(NX):
            term = dot_nn(act[m, xx], ks[src, 2 * xx : 2 * xx + 2].reshape(2 * TOK, D))
            total = term if total is None else total + term
        rys[m] = total.astype(BF16).reshape(NY, BLK, D)
        for k in (2, 1, 3):
            send(rys.at[m, (y + k) % NY], ryr.at[m, k - 1], s_ry, r_ry.at[m], ys[k])

    unp[:, :, BLK:, :] = jnp.zeros((3, 6, 8, 128), F32)
    for m in order:
        wait(ryr.at[m], r_ry.at[m])
        total = rys[m, y].astype(F32)
        for k in range(NY - 1):
            total = total + ryr[m, k].astype(F32)
        for j in range(6):
            unp[m, j, :BLK, :] = total[:, j * 128 : (j + 1) * 128]
        for zz in range(NZ):
            rzs[m, zz] = unp[m, :, zz * ROWS : zz * ROWS + 8, :].reshape(PACK, 128).astype(BF16)
        for k in (4, 3, 5, 2, 6, 1, 7):
            send(rzs.at[m, (z + k) % NZ], rzr.at[m, k - 1], s_rz, r_rz.at[m], zs[k])

    for m in order:
        wait(rzr.at[m], r_rz.at[m])
        grad = rzs[m, z].astype(F32)
        for k in range(NZ - 1):
            grad = grad + rzr[m, k].astype(F32)
        old = wpk[m].reshape(6, 8, 128)
        stepped = old - grad.reshape(6, 8, 128)
        old_ms = jnp.sum(jnp.sum(old * old, axis=0), axis=-1, keepdims=True) * (1.0 / D)
        new_ms = jnp.sum(jnp.sum(stepped * stepped, axis=0), axis=-1, keepdims=True) * (1.0 / D)
        upd = stepped * jnp.sqrt(old_ms + EPS)[None] / jnp.sqrt(new_ms + EPS)[None]
        az1[m, z] = upd.reshape(PACK, 128).astype(BF16)
        for k in (4, 3, 5, 2, 6, 1, 7):
            send(az1.at[m, z], az1.at[m, z], s_az, r_az.at[m], zs[k])

    for m in order:
        wait(az1.at[m, pl.ds(0, NZ - 1)], r_az.at[m])
        def put_new(j, v, m=m):
            wu[m, c, y, :, j * 128 : (j + 1) * 128] = v
        unpack(m, lambda zz, m=m: az1[m, zz], put_new)
        for k in (2, 1, 3):
            send(wu.at[m, c, y], wu.at[m, c, y], s_ay, r_ay.at[m], ys[k])

    for m in order:
        wait(wu.at[m, c, pl.ds(0, NY - 1)], r_ay.at[m])
        send(wu.at[m, c], wu.at[m, c], s_ac, r_ac.at[m], other)

    wait(qn.at[pl.ds(0, NX - 1)], r_q)
    hid = 2 * NY * BLK
    for m in (0, 1):
        wait(wu.at[m, 1 - c], r_ac.at[m])
        gu[m] = dot_nt(qn[...].reshape(NX * TOK, D), wu[m].reshape(hid, D))
    gate = gu[0]
    hid_q[...] = (gate * jax.nn.sigmoid(gate) * gu[1]).astype(BF16)
    wait(wu.at[2, 1 - c], r_ac.at[2])
    part = dot_nn(hid_q[...], wu[2].reshape(hid, D)).reshape(NX, TOK, D)
    fo[...] = part
    ps[...] = part.astype(BF16)
    for k in (2, 1, 3):
        send(ps.at[(x + k) % NX], pr.at[k - 1], s_p, r_p, xs[k])

    wait(az0.at[pl.ds(0, NZ - 1)], s_az0)
    for k in range(NX - 1):
        wait(ks.at[:, 0], s_tok.at[k])
    for k in range(NX):
        wait(ks.at[:, 0], s_tokc.at[k])
    wait(w.at[:, pl.ds(0, NY - 1)], s_wy)
    wait(qn.at[pl.ds(0, NX - 1)], s_q)
    wait(ryr, s_ry)
    wait(rzr, s_rz)
    wait(az1.at[:, pl.ds(0, NZ - 1)], s_az)
    wait(wu.at[:, 0, pl.ds(0, NY - 1)], s_ay)
    wait(wu.at[:, 0], s_ac)
    wait(pr, s_p)

    wait(pr, r_p)
    result = fo[x] + att[...]
    for k in range(NX - 1):
        result = result + pr[k].astype(F32)
    out_ref[...] = result.astype(BF16)


def body(key_tokens, value_tokens, queries, token_rate, fast_weights):
    vmem = pl.BlockSpec(memory_space=pltpu.VMEM)
    dma = pltpu.SemaphoreType.DMA
    return pl.pallas_call(
        kernel,
        name="ttt_layer",
        out_shape=jax.ShapeDtypeStruct((TOK, D), BF16),
        in_specs=[vmem] * 5,
        out_specs=vmem,
        scratch_shapes=[
            pltpu.VMEM((3, PACK, 128), F32),
            pltpu.VMEM((NZ, 3, PACK, 128), BF16),
            pltpu.VMEM((3, NY, BLK, D), BF16),
            pltpu.VMEM((2, 2 * NX, TOK, D), BF16),
            pltpu.VMEM((NX, TOK, D), BF16),
            pltpu.VMEM((3, NX, NY * BLK, 2 * TOK), BF16),
            pltpu.VMEM((3, NY, BLK, D), BF16),
            pltpu.VMEM((3, NY - 1, BLK, D), BF16),
            pltpu.VMEM((3, NZ, PACK, 128), BF16),
            pltpu.VMEM((3, NZ - 1, PACK, 128), BF16),
            pltpu.VMEM((3, NZ, PACK, 128), BF16),
            pltpu.VMEM((3, 2, NY, BLK, D), BF16),
            pltpu.VMEM((3, 6, BLK + 8, 128), F32),
            pltpu.VMEM((2, NX * TOK, 2 * NY * BLK), F32),
            pltpu.VMEM((NX * TOK, 2 * NY * BLK), BF16),
            pltpu.VMEM((NX, TOK, D), F32),
            pltpu.VMEM((NX, TOK, D), BF16),
            pltpu.VMEM((NX - 1, TOK, D), BF16),
            pltpu.VMEM((TOK, D), F32),
            dma, dma, dma, dma,
            dma((NX - 1,)), dma((NX - 1,)), dma((NX,)), dma((NX,)), dma, dma,
            dma, dma((3,)), dma, dma((3,)), dma, dma((3,)), dma, dma((3,)), dma, dma((3,)),
            dma, dma,
        ],
        compiler_params=pltpu.CompilerParams(
            collective_id=0, has_side_effects=True, vmem_limit_bytes=48 << 20
        ),
    )(key_tokens, value_tokens, queries, token_rate.reshape(TOK, 1), fast_weights)


def solution(mesh):
    rows = P(("grp", "dev"), None)
    in_specs = (rows, rows, rows, P(("grp", "dev")), P(None, ("grp", "dev"), None))
    return jax.shard_map(body, mesh=mesh, in_specs=in_specs, out_specs=rows, check_vma=False)
```

time: 1850 us -> 81.1 us (0.04)
  waiting for transfers between devices: 1750 us -> 0 us
  Pallas kernels: 0 us -> 76.6 us
  blocking collectives: 33.2 us -> 0 us
  local copies, waits for them, and re-layouts: 30.2 us -> 4.24 us
    all_gather x2 -> x0, waiting for transfers between devices: 1040 us -> none  [the longest x1 761 us: body(): shard_rows = lax.all_gather(updated, ('grp', 'dev'), axis=1, tiled=True)]
    unnamed x4 -> x0, waiting for transfers between devices: 716 us -> none
    pallas_call x0 -> x1, Pallas kernels: none -> 76.6 us  [body(): pl.pallas_call(kernel, name='ttt_layer', out_shape=jax.ShapeDtypeStruct((...]
    all_gather x2 -> x0, blocking collectives: 33.2 us -> none  [the longest x1 17.2 us: body(): lax.all_gather(key_normed, 'grp', axis=0, tiled=True)]
    slice x2 -> x0, local copies, waits for them, and re-layouts: 26.4 us -> none  [the longest x1 19.9 us: body(): shard_rows[0]]
  transfers between devices with their start and end apart: 3 -> 0, of which waited for: 3 -> 0; matrix products, arithmetic and copies ran while one was open for 0% -> 0% of each run, Pallas kernels for 0% -> 0%
where the time goes in v1:
time: 81.1 us; the launch traced here: 80.9 us
  Pallas kernels  76.6 us (94%)
  local copies, waits for them, and re-layouts  4.24 us (5%)
    pallas_call x1, Pallas kernels, body(): pl.pallas_call(kernel, name='ttt_layer', out_shape=jax.ShapeDtypeStruct((...  76.6 us
    unnamed x9, local copies, waits for them, and re-layouts  3.47 us

profile of v1, /device:TPU:1, one launch (start us, length us, event | category | flops | bytes accessed | tf_op | source)
XLA Modules:
  0.0 80.9 jit_solution(9628751367140960499)
XLA Ops:
  0.0 0.0 copy-start.3
  0.0 0.8 copy.6.rate_ref
  0.8 0.0 copy-done.3
  0.8 0.0 copy-start
  0.8 0.9 %copy-done = bf16[128,768]{1,0:T(8,128)(2,1)S(1)} copy-done((bf16[128,768]{1,0:T(8,128)(2,1)S(1)}, bf16[128,768]{1,0:T(8,128)(2,1)}, u32[]{:S(2)}) %copy-start) | copy-done | bytes 196632
  1.7 0.0 copy-start.1
  1.7 0.9 %copy-done.1 = bf16[128,768]{1,0:T(8,128)(2,1)S(1)} copy-done((bf16[128,768]{1,0:T(8,128)(2,1)S(1)}, bf16[128,768]{1,0:T(8,128)(2,1)}, u32[]{:S(2)}) %copy-start.1) | copy-done | bytes 196632
  2.6 0.0 copy-start.2
  2.6 0.9 %copy-done.2 = bf16[128,768]{1,0:T(8,128)(2,1)S(1)} copy-done((bf16[128,768]{1,0:T(8,128)(2,1)S(1)}, bf16[128,768]{1,0:T(8,128)(2,1)}, u32[]{:S(2)}) %copy-start.2) | copy-done | bytes 196632
  3.6 76.6 %ttt_layer.1 = bf16[128,768]{1,0:T(8,128)(2,1)S(1)} custom-call(bf16[128,768]{1,0:T(8,128)(2,1)S(1)} %copy-done, bf16[128,768]{1,0:T(8,128)(2,1)S(1)} %copy-done.1, bf16[128,768]{1,0:T(8,128)(2,1)S(1)} %copy-done.2, f32[128,1]{1,0:T(8,128)S(1)} %copy.6.rate_ref, bf16[3,6,768]{2,1,0:T(8,128)(2,1)S(1)} %copy-done.3), custom_call_target="tpu_custom_call" | custom-call | tf_op jit(solution)/shard_map/ttt_layer/pallas_call | solution.py:227
  80.2 0.7 copy.8
Async XLA Ops:
  0.0 0.8 copy-start.3
  0.8 0.9 %copy-start = (bf16[128,768]{1,0:T(8,128)(2,1)S(1)}, bf16[128,768]{1,0:T(8,128)(2,1)}, u32[]{:S(2)}) copy-start(bf16[128,768]{1,0:T(8,128)(2,1)} %key_ref.1) | copy-start | bytes 589828
  1.7 0.9 %copy-start.1 = (bf16[128,768]{1,0:T(8,128)(2,1)S(1)}, bf16[128,768]{1,0:T(8,128)(2,1)}, u32[]{:S(2)}) copy-start(bf16[128,768]{1,0:T(8,128)(2,1)} %val_ref.1) | copy-start | bytes 589828
  2.6 0.9 %copy-start.2 = (bf16[128,768]{1,0:T(8,128)(2,1)S(1)}, bf16[128,768]{1,0:T(8,128)(2,1)}, u32[]{:S(2)}) copy-start(bf16[128,768]{1,0:T(8,128)(2,1)} %qry_ref.1) | copy-start | bytes 589828

commit v2 on v1

v2 whole, which is shorter than its diff:
```python
import functools

import jax
import jax.numpy as jnp
from jax import lax
from jax.experimental import pallas as pl
from jax.experimental.pallas import tpu as pltpu
from jax.sharding import PartitionSpec as P

D = 768
TOK = 128
EPS = 1e-06
NX, NY, NZ = 4, 4, 8
ROWS = 6
BLK = NZ * ROWS
PACK = 48
MESH = pl.DeviceIdType.MESH
F32 = jnp.float32
BF16 = jnp.bfloat16


def dot_nt(a, b):
    return lax.dot_general(a, b, (((1,), (1,)), ((), ())), preferred_element_type=F32)


def dot_nn(a, b):
    return lax.dot_general(a, b, (((1,), (0,)), ((), ())), preferred_element_type=F32)


def device(x, y, z, c):
    return ((z // 4) * 2 + c, (z % 4) * 16 + y * 4 + x)


def rms_scale(rows):
    return lax.rsqrt(jnp.mean(rows * rows, axis=-1, keepdims=True) + EPS)


def kernel(
    key_hbm, val_hbm, qry_hbm, rate_hbm, w_hbm, out_ref,
    key_ref, val_ref, qry_ref, rate_ref, w_ref,
    wpk, az0, w, ks, qn, gs, act, rys, ryr, rzs, rzr, az1, wu, unp, gu, hid_q, ps, pr, att,
    s_in, s_az0, r_az0, s_wy, r_wy, s_tok, r_tok, r_tokc, s_q, r_q,
    s_ry, r_ry, s_rz, r_rz, s_az, r_az, s_ay, r_ay, s_ac, r_ac, s_p, r_p,
):
    g = lax.axis_index("grp")
    d = lax.axis_index("dev")
    x, y, z, c = d % 4, (d // 4) % 4, (g // 2) * 4 + d // 16, g % 2
    other = device(x, y, z, 1 - c)
    xs = [device((x + k) % NX, y, z, c) for k in range(NX)]
    ys = [device(x, (y + k) % NY, z, c) for k in range(NY)]
    zs = [device(x, y, (z + k) % NZ, c) for k in range(NZ)]
    far_first_z = (4, 3, 5, 2, 6, 1, 7)

    barrier = pltpu.get_barrier_semaphore()
    peers = [other] + xs[1:] + ys[1:] + zs[1:]
    for peer in peers:
        pl.semaphore_signal(barrier, inc=1, device_id=peer, device_id_type=MESH)

    fetches = [
        pltpu.make_async_copy(src, dst, s_in.at[i])
        for i, (src, dst) in enumerate(
            [(w_hbm, w_ref), (key_hbm, key_ref), (val_hbm, val_ref), (rate_hbm, rate_ref), (qry_hbm, qry_ref)]
        )
    ]
    for fetch in fetches:
        fetch.start()

    def send(src, dst, ssem, rsem, peer):
        pltpu.make_async_remote_copy(
            src_ref=src, dst_ref=dst, send_sem=ssem, recv_sem=rsem, device_id=peer, device_id_type=MESH
        ).start()

    def wait(ref, sem):
        pltpu.make_async_copy(ref, ref, sem).wait()

    wpk[...] = jnp.zeros_like(wpk)
    fetches[0].wait()
    for m in range(3):
        rows = w_ref[m].astype(F32)
        for j in range(6):
            wpk[m, j * 8 : j * 8 + ROWS, :] = rows[:, j * 128 : (j + 1) * 128]
        az0[m, z] = wpk[m].astype(BF16)

    slot = x * 2 + c
    fetches[1].wait()
    keys = key_ref[...].astype(F32)
    ks[0, slot] = (keys * rms_scale(keys)).astype(BF16)
    fetches[2].wait()
    fetches[3].wait()
    diagonal = lax.broadcasted_iota(jnp.int32, (TOK, TOK), 0) == lax.broadcasted_iota(jnp.int32, (TOK, TOK), 1)
    rate = jnp.sum(jnp.where(diagonal, rate_ref[...], 0.0), axis=-1, keepdims=True)
    ks[1, slot] = (-(rate * val_ref[...].astype(F32))).astype(BF16)

    pl.semaphore_wait(barrier, len(peers))

    def send_tok(kind, sl, sem, peer):
        send(ks.at[kind, sl], ks.at[kind, sl], s_tok, sem, peer)
    for k in far_first_z:
        send(az0.at[0, z], az0.at[0, z], s_az0, r_az0.at[0], zs[k])
    send_tok(0, slot, r_tok.at[0, 0], xs[1])
    send_tok(1, slot, r_tok.at[2, 1], xs[3])
    send_tok(1, slot, r_tok.at[0, 1], xs[1])
    send_tok(0, slot, r_tok.at[2, 0], xs[3])
    for kind in range(2):
        send_tok(kind, slot, r_tokc.at[0, kind], other)
    for m in (1, 2):
        for k in far_first_z:
            send(az0.at[m, z], az0.at[m, z], s_az0, r_az0.at[m], zs[k])
    fetches[4].wait()
    queries = qry_ref[...].astype(F32)
    qn[x] = (queries * rms_scale(queries)).astype(BF16)

    def token_slot(k, core):
        return ((x + NX - k) % NX) * 2 + core

    def tokens_in(k, kind, onward):
        sl = token_slot(k, c)
        wait(ks.at[kind, sl], r_tok.at[k - 1, kind])
        if onward is not None:
            send_tok(kind, sl, r_tok.at[1, kind], onward)
        send_tok(kind, sl, r_tokc.at[k, kind], other)

    def unpack(m, packed, store):
        for zz in range(NZ):
            unp[m, :, zz * ROWS : zz * ROWS + 8, :] = packed[m, zz].astype(F32).reshape(6, 8, 128)
        for j in range(6):
            store(j, unp[m, j, :BLK, :].astype(BF16))

    def old_weights(m):
        wait(az0.at[m, pl.ds(0, NZ - 1)], r_az0.at[m])
        def put(j, v):
            w[m, y, :, j * 128 : (j + 1) * 128] = v
        unpack(m, az0, put)
        for k in (2, 1, 3):
            send(w.at[m, y], w.at[m, y], s_wy, r_wy.at[m], ys[k])

    old_weights(0)
    old_weights(1)
    tokens_in(1, 0, xs[1])
    tokens_in(3, 1, xs[3])
    old_weights(2)

    lane = lax.broadcasted_iota(jnp.int32, (TOK, 128), 1)
    for p in range(6):
        cols = slice(p * 128, (p + 1) * 128)
        qp, kp, vp = qry_ref[:, cols], key_ref[:, cols], val_ref[:, cols]
        zero = jnp.zeros_like(qp)
        both = jnp.concatenate([jnp.where(lane < 64, qp, zero), jnp.where(lane < 64, zero, qp)], axis=0)
        scores = dot_nt(both, kp) * 0.125
        e = jnp.exp(scores - jnp.max(scores, axis=-1, keepdims=True))
        probs = (e / jnp.sum(e, axis=-1, keepdims=True)).astype(BF16)
        mixed = dot_nn(probs, vp)
        att[:, cols] = jnp.where(lane < 64, mixed[:TOK], mixed[TOK:])

    tokens_in(1, 1, None)
    tokens_in(3, 0, None)

    def chunk(kind, k):
        xx = (x + NX - k) % NX
        return ks[kind, pl.ds(xx * 2, 2)].reshape(2 * TOK, D)

    def forward(k):
        wait(ks.at[0, 0], r_tokc.at[k, 0])
        kn = chunk(0, k)
        gate = dot_nt(w[0].reshape(NY * BLK, D), kn)
        up = dot_nt(w[1].reshape(NY * BLK, D), kn)
        gs[0, k] = gate
        gs[1, k] = up
        act[2, k] = (gate * jax.nn.sigmoid(gate) * up).astype(BF16)

    def backward(k):
        hgrad = dot_nt(w[2].reshape(NY * BLK, D), chunk(1, k))
        gate, up = gs[0, k], gs[1, k]
        sig = jax.nn.sigmoid(gate)
        act[0, k] = (hgrad * up * sig * (1.0 + gate * (1.0 - sig))).astype(BF16)
        act[1, k] = (hgrad * (gate * sig)).astype(BF16)

    wait(w.at[0, pl.ds(0, NY - 1)], r_wy.at[0])
    wait(w.at[1, pl.ds(0, NY - 1)], r_wy.at[1])
    for k in (0, 1, 3):
        forward(k)
    tokens_in(2, 0, None)
    tokens_in(2, 1, None)
    for k in (2, 1, 3):
        send(qn.at[x], qn.at[x], s_q, r_q, xs[k])
    forward(2)
    for k in (0, 1, 3, 2):
        wait(ks.at[1, 0], r_tokc.at[k, 1])

    def gradient(m):
        total = None
        for k in range(NX):
            term = dot_nn(act[m, k], chunk(1 if m == 2 else 0, k))
            total = term if total is None else total + term
        rys[m] = total.astype(BF16).reshape(NY, BLK, D)
        for k in (2, 1, 3):
            send(rys.at[m, (y + k) % NY], ryr.at[m, k - 1], s_ry, r_ry.at[m], ys[k])

    gradient(2)
    wait(w.at[2, pl.ds(0, NY - 1)], r_wy.at[2])
    for k in (0, 1, 3, 2):
        backward(k)
    gradient(0)
    gradient(1)

    order = (2, 0, 1)
    unp[:, :, BLK:, :] = jnp.zeros((3, 6, 8, 128), F32)
    for m in order:
        wait(ryr.at[m], r_ry.at[m])
        total = rys[m, y].astype(F32)
        for k in range(NY - 1):
            total = total + ryr[m, k].astype(F32)
        for j in range(6):
            unp[m, j, :BLK, :] = total[:, j * 128 : (j + 1) * 128]
        for zz in range(NZ):
            rzs[m, zz] = unp[m, :, zz * ROWS : zz * ROWS + 8, :].reshape(PACK, 128).astype(BF16)
        for k in far_first_z:
            send(rzs.at[m, (z + k) % NZ], rzr.at[m, k - 1], s_rz, r_rz.at[m], zs[k])

    for m in order:
        wait(rzr.at[m], r_rz.at[m])
        grad = rzs[m, z].astype(F32)
        for k in range(NZ - 1):
            grad = grad + rzr[m, k].astype(F32)
        old = wpk[m].reshape(6, 8, 128)
        stepped = old - grad.reshape(6, 8, 128)
        old_ms = jnp.sum(jnp.sum(old * old, axis=0), axis=-1, keepdims=True) * (1.0 / D)
        new_ms = jnp.sum(jnp.sum(stepped * stepped, axis=0), axis=-1, keepdims=True) * (1.0 / D)
        upd = stepped * jnp.sqrt(old_ms + EPS)[None] / jnp.sqrt(new_ms + EPS)[None]
        az1[m, z] = upd.reshape(PACK, 128).astype(BF16)
        for k in far_first_z:
            send(az1.at[m, z], az1.at[m, z], s_az, r_az.at[m], zs[k])

    for m in order:
        wait(az1.at[m, pl.ds(0, NZ - 1)], r_az.at[m])
        def put_new(j, v, m=m):
            wu[m, c, y, :, j * 128 : (j + 1) * 128] = v
        unpack(m, az1, put_new)
        for k in (2, 1, 3):
            send(wu.at[m, c, y], wu.at[m, c, y], s_ay, r_ay.at[m], ys[k])

    wait(qn.at[pl.ds(0, NX - 1)], r_q)
    for m in order:
        wait(wu.at[m, c, pl.ds(0, NY - 1)], r_ay.at[m])
        send(wu.at[m, c], wu.at[m, c], s_ac, r_ac.at[m], other)
        if m < 2:
            gu[m, 0] = dot_nt(qn[...].reshape(NX * TOK, D), wu[m, c].reshape(NY * BLK, D))

    def query_hidden(half):
        gate = gu[0, half]
        hid_q[half] = (gate * jax.nn.sigmoid(gate) * gu[1, half]).astype(BF16).reshape(NX, TOK, NY * BLK)

    query_hidden(0)
    for m in (0, 1):
        wait(wu.at[m, 1 - c], r_ac.at[m])
        gu[m, 1] = dot_nt(qn[...].reshape(NX * TOK, D), wu[m, 1 - c].reshape(NY * BLK, D))
    query_hidden(1)
    wait(wu.at[2, 1 - c], r_ac.at[2])
    down_own = wu[2, c].reshape(NY * BLK, D)
    down_other = wu[2, 1 - c].reshape(NY * BLK, D)
    for k in (2, 1, 3, 0):
        to = (x + k) % NX
        part = dot_nn(hid_q[0, to], down_own) + dot_nn(hid_q[1, to], down_other)
        if k:
            ps[k - 1] = part.astype(BF16)
            send(ps.at[k - 1], pr.at[k - 1], s_p, r_p, xs[k])
        else:
            att[...] += part

    wait(az0.at[:, pl.ds(0, NZ - 1)], s_az0)
    for _ in range(7):
        wait(ks.at[:, 0], s_tok)
    wait(w.at[:, pl.ds(0, NY - 1)], s_wy)
    wait(qn.at[pl.ds(0, NX - 1)], s_q)
    wait(ryr, s_ry)
    wait(rzr, s_rz)
    wait(az1.at[:, pl.ds(0, NZ - 1)], s_az)
    wait(wu.at[:, 0, pl.ds(0, NY - 1)], s_ay)
    wait(wu.at[:, 0], s_ac)
    wait(pr, s_p)

    wait(pr, r_p)
    result = att[...]
    for k in range(NX - 1):
        result = result + pr[k].astype(F32)
    out_ref[...] = result.astype(BF16)


def body(key_tokens, value_tokens, queries, token_rate, fast_weights):
    vmem = pltpu.VMEM
    dma = pltpu.SemaphoreType.DMA
    return pl.pallas_call(
        kernel,
        name="ttt_layer",
        out_shape=jax.ShapeDtypeStruct((TOK, D), BF16),
        in_specs=[pl.BlockSpec(memory_space=pl.ANY)] * 5,
        out_specs=pl.BlockSpec(memory_space=pltpu.VMEM),
        scratch_shapes=[
            vmem((TOK, D), BF16),
            vmem((TOK, D), BF16),
            vmem((TOK, D), BF16),
            vmem((1, TOK), F32),
            vmem((3, ROWS, D), BF16),
            vmem((3, PACK, 128), F32),
            vmem((3, NZ, PACK, 128), BF16),
            vmem((3, NY, BLK, D), BF16),
            vmem((2, 2 * NX, TOK, D), BF16),
            vmem((NX, TOK, D), BF16),
            vmem((2, NX, NY * BLK, 2 * TOK), F32),
            vmem((3, NX, NY * BLK, 2 * TOK), BF16),
            vmem((3, NY, BLK, D), BF16),
            vmem((3, NY - 1, BLK, D), BF16),
            vmem((3, NZ, PACK, 128), BF16),
            vmem((3, NZ - 1, PACK, 128), BF16),
            vmem((3, NZ, PACK, 128), BF16),
            vmem((3, 2, NY, BLK, D), BF16),
            vmem((3, 6, BLK + 8, 128), F32),
            vmem((2, 2, NX * TOK, NY * BLK), F32),
            vmem((2, NX, TOK, NY * BLK), BF16),
            vmem((NX - 1, TOK, D), BF16),
            vmem((NX - 1, TOK, D), BF16),
            vmem((TOK, D), F32),
            dma((5,)), dma, dma((3,)), dma, dma((3,)), dma, dma((3, 2)), dma((NX, 2)), dma, dma,
            dma, dma((3,)), dma, dma((3,)), dma, dma((3,)), dma, dma((3,)), dma, dma((3,)),
            dma, dma,
        ],
        compiler_params=pltpu.CompilerParams(
            collective_id=0, has_side_effects=True, vmem_limit_bytes=56 << 20
        ),
    )(key_tokens, value_tokens, queries, token_rate.reshape(1, TOK), fast_weights)


def solution(mesh):
    rows = P(("grp", "dev"), None)
    in_specs = (rows, rows, rows, P(("grp", "dev")), P(None, ("grp", "dev"), None))
    return jax.shard_map(body, mesh=mesh, in_specs=in_specs, out_specs=rows, check_vma=False)
```

time: 81.1 us -> 74.5 us (0.919)
  Pallas kernels: 76.6 us -> 72.7 us
  local copies, waits for them, and re-layouts: 4.24 us -> 1.62 us
    pallas_call x1, Pallas kernels: 76.6 us -> 72.7 us  [body(): pl.pallas_call(kernel, name='ttt_layer', out_shape=jax.ShapeDtypeStruct((...]
    unnamed x9 -> x1, local copies, waits for them, and re-layouts: 3.47 us -> 1.62 us
where the time goes in v2:
time: 74.5 us; the launch traced here: 74.4 us
  Pallas kernels  72.7 us (98%)
  local copies, waits for them, and re-layouts  1.62 us (2%)
    pallas_call x1, Pallas kernels, body(): pl.pallas_call(kernel, name='ttt_layer', out_shape=jax.ShapeDtypeStruct((...  72.7 us
    unnamed x1, local copies, waits for them, and re-layouts  1.62 us

profile of v2, /device:TPU:1, one launch (start us, length us, event | category | flops | bytes accessed | tf_op | source)
XLA Modules:
  0.0 74.4 jit_solution(13945635730294547389)
XLA Ops:
  0.0 72.7 %ttt_layer.1 = bf16[128,768]{1,0:T(8,128)(2,1)} custom-call(bf16[128,768]{1,0:T(8,128)(2,1)} %key_hbm.1, bf16[128,768]{1,0:T(8,128)(2,1)} %val_hbm.1, bf16[128,768]{1,0:T(8,128)(2,1)} %qry_hbm.1, f32[1,128]{1,0:T(1,128)} %bitcast.1, bf16[3,6,768]{2,1,0:T(8,128)(2,1)} %w_hbm.1), custom_call_target="tpu_custom_call" | custom-call | tf_op jit(solution)/shard_map/ttt_layer/pallas_call | solution.py:292
  72.7 1.6 %copy.7 = bf16[128,768]{1,0:T(8,128)(2,1)} copy(bf16[128,768]{1,0:T(8,128)(2,1)} %ttt_layer.1) | data formatting | bytes 393216

commit v3 on v2

--- a/solution.py
+++ b/solution.py
@@ -49,6 +49,11 @@
     xs = [device((x + k) % NX, y, z, c) for k in range(NX)]
     ys = [device(x, (y + k) % NY, z, c) for k in range(NY)]
     zs = [device(x, y, (z + k) % NZ, c) for k in range(NZ)]
+    pos = (y * (1 - c) + x * c, x * (1 - c) + y * c)
+    lines = (
+        [device((x + k * c) % NX, (y + k * (1 - c)) % NY, z, c) for k in range(NX)],
+        [device((x + k * (1 - c)) % NX, (y + k * c) % NY, z, c) for k in range(NX)],
+    )
     far_first_z = (4, 3, 5, 2, 6, 1, 7)
 
     barrier = pltpu.get_barrier_semaphore()
@@ -108,7 +113,9 @@
             send(az0.at[m, z], az0.at[m, z], s_az0, r_az0.at[m], zs[k])
     fetches[4].wait()
     queries = qry_ref[...].astype(F32)
-    qn[x] = (queries * rms_scale(queries)).astype(BF16)
+    normed = (queries * rms_scale(queries)).astype(BF16)
+    qn[0, x] = normed
+    qn[1, y] = normed
 
     def token_slot(k, core):
         return ((x + NX - k) % NX) * 2 + core
@@ -182,7 +189,7 @@
     tokens_in(2, 0, None)
     tokens_in(2, 1, None)
     for k in (2, 1, 3):
-        send(qn.at[x], qn.at[x], s_q, r_q, xs[k])
+        send(qn.at[0, x], qn.at[0, x], s_q, r_q.at[0], xs[k])
     forward(2)
     for k in (0, 1, 3, 2):
         wait(ks.at[1, 0], r_tokc.at[k, 1])
@@ -202,6 +209,8 @@
         backward(k)
     gradient(0)
     gradient(1)
+    for k in (2, 1, 3):
+        send(qn.at[1, y], qn.at[1, y], s_q, r_q.at[1], ys[k])
 
     order = (2, 0, 1)
     unp[:, :, BLK:, :] = jnp.zeros((3, 6, 8, 128), F32)
@@ -234,44 +243,49 @@
     for m in order:
         wait(az1.at[m, pl.ds(0, NZ - 1)], r_az.at[m])
         def put_new(j, v, m=m):
-            wu[m, c, y, :, j * 128 : (j + 1) * 128] = v
+            wu[m, c, pos[0], :, j * 128 : (j + 1) * 128] = v
         unpack(m, az1, put_new)
         for k in (2, 1, 3):
-            send(wu.at[m, c, y], wu.at[m, c, y], s_ay, r_ay.at[m], ys[k])
-
-    wait(qn.at[pl.ds(0, NX - 1)], r_q)
+            send(wu.at[m, c, pos[0]], wu.at[m, c, pos[0]], s_ay, r_ay.at[m], lines[0][k])
+
+    def project(m, half, core):
+        gu[m, half] = dot_nt(qn[core].reshape(NX * TOK, D), wu[m, core].reshape(NY * BLK, D))
+
+    def query_hidden(half):
+        gate = gu[0, half]
+        hid_q[half] = (gate * jax.nn.sigmoid(gate) * gu[1, half]).astype(BF16).reshape(NX, TOK, NY * BLK)
+
+    def partial_outputs(half, core):
+        down = wu[2, core].reshape(NY * BLK, D)
+        for k in (2, 1, 3, 0):
+            part = dot_nn(hid_q[half, (pos[1 - half] + k) % NX], down)
+            if k:
+                ps[half, k - 1] = part.astype(BF16)
+                send(ps.at[half, k - 1], pr.at[half, k - 1], s_p, r_p.at[half], lines[1 - half][k])
+            else:
+                att[...] += part
+
+    for axis in range(2):
+        wait(qn.at[axis, pl.ds(0, NX - 1)], r_q.at[axis])
     for m in order:
         wait(wu.at[m, c, pl.ds(0, NY - 1)], r_ay.at[m])
         send(wu.at[m, c], wu.at[m, c], s_ac, r_ac.at[m], other)
         if m < 2:
-            gu[m, 0] = dot_nt(qn[...].reshape(NX * TOK, D), wu[m, c].reshape(NY * BLK, D))
-
-    def query_hidden(half):
-        gate = gu[0, half]
-        hid_q[half] = (gate * jax.nn.sigmoid(gate) * gu[1, half]).astype(BF16).reshape(NX, TOK, NY * BLK)
-
+            project(m, 0, c)
     query_hidden(0)
+    partial_outputs(0, c)
     for m in (0, 1):
         wait(wu.at[m, 1 - c], r_ac.at[m])
-        gu[m, 1] = dot_nt(qn[...].reshape(NX * TOK, D), wu[m, 1 - c].reshape(NY * BLK, D))
+        project(m, 1, 1 - c)
     query_hidden(1)
     wait(wu.at[2, 1 - c], r_ac.at[2])
-    down_own = wu[2, c].reshape(NY * BLK, D)
-    down_other = wu[2, 1 - c].reshape(NY * BLK, D)
-    for k in (2, 1, 3, 0):
-        to = (x + k) % NX
-        part = dot_nn(hid_q[0, to], down_own) + dot_nn(hid_q[1, to], down_other)
-        if k:
-            ps[k - 1] = part.astype(BF16)
-            send(ps.at[k - 1], pr.at[k - 1], s_p, r_p, xs[k])
-        else:
-            att[...] += part
+    partial_outputs(1, 1 - c)
 
     wait(az0.at[:, pl.ds(0, NZ - 1)], s_az0)
     for _ in range(7):
         wait(ks.at[:, 0], s_tok)
     wait(w.at[:, pl.ds(0, NY - 1)], s_wy)
-    wait(qn.at[pl.ds(0, NX - 1)], s_q)
+    wait(qn.at[:, pl.ds(0, NX - 1)], s_q)
     wait(ryr, s_ry)
     wait(rzr, s_rz)
     wait(az1.at[:, pl.ds(0, NZ - 1)], s_az)
@@ -279,10 +293,11 @@
     wait(wu.at[:, 0], s_ac)
     wait(pr, s_p)
 
-    wait(pr, r_p)
     result = att[...]
-    for k in range(NX - 1):
-        result = result + pr[k].astype(F32)
+    for half in range(2):
+        wait(pr.at[half], r_p.at[half])
+        for k in range(NX - 1):
+            result = result + pr[half, k].astype(F32)
     out_ref[...] = result.astype(BF16)
 
 
@@ -305,7 +320,7 @@
             vmem((3, NZ, PACK, 128), BF16),
             vmem((3, NY, BLK, D), BF16),
             vmem((2, 2 * NX, TOK, D), BF16),
-            vmem((NX, TOK, D), BF16),
+            vmem((2, NX, TOK, D), BF16),
             vmem((2, NX, NY * BLK, 2 * TOK), F32),
             vmem((3, NX, NY * BLK, 2 * TOK), BF16),
             vmem((3, NY, BLK, D), BF16),
@@ -317,12 +332,12 @@
             vmem((3, 6, BLK + 8, 128), F32),
             vmem((2, 2, NX * TOK, NY * BLK), F32),
             vmem((2, NX, TOK, NY * BLK), BF16),
-            vmem((NX - 1, TOK, D), BF16),
-            vmem((NX - 1, TOK, D), BF16),
+            vmem((2, NX - 1, TOK, D), BF16),
+            vmem((2, NX - 1, TOK, D), BF16),
             vmem((TOK, D), F32),
-            dma((5,)), dma, dma((3,)), dma, dma((3,)), dma, dma((3, 2)), dma((NX, 2)), dma, dma,
+            dma((5,)), dma, dma((3,)), dma, dma((3,)), dma, dma((3, 2)), dma((NX, 2)), dma, dma((2,)),
             dma, dma((3,)), dma, dma((3,)), dma, dma((3,)), dma, dma((3,)), dma, dma((3,)),
-            dma, dma,
+            dma, dma((2,)),
         ],
         compiler_params=pltpu.CompilerParams(
             collective_id=0, has_side_effects=True, vmem_limit_bytes=56 << 20

time: 74.5 us -> 69.7 us (0.936)
  Pallas kernels: 72.7 us -> 68 us
    pallas_call x1, Pallas kernels: 72.7 us -> 68 us  [body(): pl.pallas_call(kernel, name='ttt_layer', out_shape=jax.ShapeDtypeStruct((...]
where the time goes in v3:
time: 69.7 us; the launch traced here: 69.6 us
  Pallas kernels  68 us (98%)
  local copies, waits for them, and re-layouts  1.62 us (2%)
    pallas_call x1, Pallas kernels, body(): pl.pallas_call(kernel, name='ttt_layer', out_shape=jax.ShapeDtypeStruct((...  68 us
    unnamed x1, local copies, waits for them, and re-layouts  1.62 us

profile of v3, /device:TPU:1, one launch (start us, length us, event | category | flops | bytes accessed | tf_op | source)
XLA Modules:
  0.0 69.6 jit_solution(16723552439172308641)
XLA Ops:
  0.0 68.0 %ttt_layer.1 = bf16[128,768]{1,0:T(8,128)(2,1)} custom-call(bf16[128,768]{1,0:T(8,128)(2,1)} %key_hbm.1, bf16[128,768]{1,0:T(8,128)(2,1)} %val_hbm.1, bf16[128,768]{1,0:T(8,128)(2,1)} %qry_hbm.1, f32[1,128]{1,0:T(1,128)} %bitcast.1, bf16[3,6,768]{2,1,0:T(8,128)(2,1)} %w_hbm.1), custom_call_target="tpu_custom_call" | custom-call | tf_op jit(solution)/shard_map/ttt_layer/pallas_call | solution.py:307
  68.0 1.6 %copy.7 = bf16[128,768]{1,0:T(8,128)(2,1)} copy(bf16[128,768]{1,0:T(8,128)(2,1)} %ttt_layer.1) | data formatting | bytes 393216

commit v4 on v3

--- a/solution.py
+++ b/solution.py
@@ -14,6 +14,7 @@
 ROWS = 6
 BLK = NZ * ROWS
 PACK = 48
+HALF = D // 2
 MESH = pl.DeviceIdType.MESH
 F32 = jnp.float32
 BF16 = jnp.bfloat16
@@ -38,9 +39,9 @@
 def kernel(
     key_hbm, val_hbm, qry_hbm, rate_hbm, w_hbm, out_ref,
     key_ref, val_ref, qry_ref, rate_ref, w_ref,
-    wpk, az0, w, ks, qn, gs, act, rys, ryr, rzs, rzr, az1, wu, unp, gu, hid_q, ps, pr, att,
+    wpk, az0, w, ks, qn, gs, act, rys, ryv, rym, ryr, rzs, rzr, az1, wu, unp, gu, hid_q, ps, pv, pm, pr, att,
     s_in, s_az0, r_az0, s_wy, r_wy, s_tok, r_tok, r_tokc, s_q, r_q,
-    s_ry, r_ry, s_rz, r_rz, s_az, r_az, s_ay, r_ay, s_ac, r_ac, s_p, r_p,
+    s_ry, r_ryv, r_ry, s_rz, r_rz, s_az, r_az, s_ay, r_ay, s_ac, r_ac, s_p, r_pv, r_p,
 ):
     g = lax.axis_index("grp")
     d = lax.axis_index("dev")
@@ -78,6 +79,22 @@
     def wait(ref, sem):
         pltpu.make_async_copy(ref, ref, sem).wait()
 
+    first, second = pl.ds(0, HALF), pl.ds(HALF, HALF)
+
+    def spread(right1, far, left1, via, got, ssem, via_sem, got_sem, right, left):
+        send(far.at[:, first], via.at[0], ssem, via_sem.at[0], right)
+        send(far.at[:, second], via.at[1], ssem, via_sem.at[1], left)
+        send(right1.at[:, second], got.at[0, :, second], ssem, got_sem, right)
+        send(left1.at[:, first], got.at[1, :, first], ssem, got_sem, left)
+
+    def hand_on(right1, left1, via, summed, got, ssem, via_sem, got_sem, right, left):
+        wait(via.at[0], via_sem.at[0])
+        summed[0] = (right1[:, :HALF].astype(F32) + via[0].astype(F32)).astype(BF16)
+        send(summed.at[0], got.at[0, :, first], ssem, got_sem, right)
+        wait(via.at[1], via_sem.at[1])
+        summed[1] = (left1[:, HALF:].astype(F32) + via[1].astype(F32)).astype(BF16)
+        send(summed.at[1], got.at[1, :, second], ssem, got_sem, left)
+
     wpk[...] = jnp.zeros_like(wpk)
     fetches[0].wait()
     for m in range(3):
@@ -95,6 +112,12 @@
     diagonal = lax.broadcasted_iota(jnp.int32, (TOK, TOK), 0) == lax.broadcasted_iota(jnp.int32, (TOK, TOK), 1)
     rate = jnp.sum(jnp.where(diagonal, rate_ref[...], 0.0), axis=-1, keepdims=True)
     ks[1, slot] = (-(rate * val_ref[...].astype(F32))).astype(BF16)
+
+    fetches[4].wait()
+    queries = qry_ref[...].astype(F32)
+    normed = (queries * rms_scale(queries)).astype(BF16)
+    qn[0, x] = normed
+    qn[1, y] = normed
 
     pl.semaphore_wait(barrier, len(peers))
 
@@ -108,14 +131,11 @@
     send_tok(0, slot, r_tok.at[2, 0], xs[3])
     for kind in range(2):
         send_tok(kind, slot, r_tokc.at[0, kind], other)
+    for k in (2, 1, 3):
+        send(qn.at[1, y], qn.at[1, y], s_q, r_q.at[1], ys[k])
     for m in (1, 2):
         for k in far_first_z:
             send(az0.at[m, z], az0.at[m, z], s_az0, r_az0.at[m], zs[k])
-    fetches[4].wait()
-    queries = qry_ref[...].astype(F32)
-    normed = (queries * rms_scale(queries)).astype(BF16)
-    qn[0, x] = normed
-    qn[1, y] = normed
 
     def token_slot(k, core):
         return ((x + NX - k) % NX) * 2 + core
@@ -200,8 +220,10 @@
             term = dot_nn(act[m, k], chunk(1 if m == 2 else 0, k))
             total = term if total is None else total + term
         rys[m] = total.astype(BF16).reshape(NY, BLK, D)
-        for k in (2, 1, 3):
-            send(rys.at[m, (y + k) % NY], ryr.at[m, k - 1], s_ry, r_ry.at[m], ys[k])
+        spread(
+            rys.at[m, (y + 1) % NY], rys.at[m, (y + 2) % NY], rys.at[m, (y + 3) % NY], ryv.at[m], ryr.at[m],
+            s_ry, r_ryv.at[m], r_ry.at[m], ys[1], ys[3],
+        )
 
     gradient(2)
     wait(w.at[2, pl.ds(0, NY - 1)], r_wy.at[2])
@@ -209,16 +231,18 @@
         backward(k)
     gradient(0)
     gradient(1)
-    for k in (2, 1, 3):
-        send(qn.at[1, y], qn.at[1, y], s_q, r_q.at[1], ys[k])
 
     order = (2, 0, 1)
+    for m in order:
+        hand_on(
+            rys.at[m, (y + 1) % NY], rys.at[m, (y + 3) % NY], ryv.at[m], rym.at[m], ryr.at[m],
+            s_ry, r_ryv.at[m], r_ry.at[m], ys[1], ys[3],
+        )
     unp[:, :, BLK:, :] = jnp.zeros((3, 6, 8, 128), F32)
     for m in order:
         wait(ryr.at[m], r_ry.at[m])
         total = rys[m, y].astype(F32)
-        for k in range(NY - 1):
-            total = total + ryr[m, k].astype(F32)
+        total = total + ryr[m, 0].astype(F32) + ryr[m, 1].astype(F32)
         for j in range(6):
             unp[m, j, :BLK, :] = total[:, j * 128 : (j + 1) * 128]
         for zz in range(NZ):
@@ -257,13 +281,13 @@
 
     def partial_outputs(half, core):
         down = wu[2, core].reshape(NY * BLK, D)
-        for k in (2, 1, 3, 0):
-            part = dot_nn(hid_q[half, (pos[1 - half] + k) % NX], down)
-            if k:
-                ps[half, k - 1] = part.astype(BF16)
-                send(ps.at[half, k - 1], pr.at[half, k - 1], s_p, r_p.at[half], lines[1 - half][k])
-            else:
-                att[...] += part
+        for k in (2, 1, 3):
+            ps[half, k - 1] = dot_nn(hid_q[half, (pos[1 - half] + k) % NX], down).astype(BF16)
+        spread(
+            ps.at[half, 0], ps.at[half, 1], ps.at[half, 2], pv.at[half], pr.at[half],
+            s_p, r_pv.at[half], r_p.at[half], lines[1 - half][1], lines[1 - half][3],
+        )
+        att[...] += dot_nn(hid_q[half, pos[1 - half]], down)
 
     for axis in range(2):
         wait(qn.at[axis, pl.ds(0, NX - 1)], r_q.at[axis])
@@ -280,24 +304,28 @@
     query_hidden(1)
     wait(wu.at[2, 1 - c], r_ac.at[2])
     partial_outputs(1, 1 - c)
+    for half in range(2):
+        hand_on(
+            ps.at[half, 0], ps.at[half, 2], pv.at[half], pm.at[half], pr.at[half],
+            s_p, r_pv.at[half], r_p.at[half], lines[1 - half][1], lines[1 - half][3],
+        )
 
     wait(az0.at[:, pl.ds(0, NZ - 1)], s_az0)
     for _ in range(7):
         wait(ks.at[:, 0], s_tok)
     wait(w.at[:, pl.ds(0, NY - 1)], s_wy)
     wait(qn.at[:, pl.ds(0, NX - 1)], s_q)
-    wait(ryr, s_ry)
+    wait(rys.at[:, pl.ds(0, NY - 1)], s_ry)
     wait(rzr, s_rz)
     wait(az1.at[:, pl.ds(0, NZ - 1)], s_az)
     wait(wu.at[:, 0, pl.ds(0, NY - 1)], s_ay)
     wait(wu.at[:, 0], s_ac)
-    wait(pr, s_p)
+    wait(ps, s_p)
 
     result = att[...]
     for half in range(2):
         wait(pr.at[half], r_p.at[half])
-        for k in range(NX - 1):
-            result = result + pr[half, k].astype(F32)
+        result = result + pr[half, 0].astype(F32) + pr[half, 1].astype(F32)
     out_ref[...] = result.astype(BF16)
 
 
@@ -324,7 +352,9 @@
             vmem((2, NX, NY * BLK, 2 * TOK), F32),
             vmem((3, NX, NY * BLK, 2 * TOK), BF16),
             vmem((3, NY, BLK, D), BF16),
-            vmem((3, NY - 1, BLK, D), BF16),
+            vmem((3, 2, BLK, HALF), BF16),
+            vmem((3, 2, BLK, HALF), BF16),
+            vmem((3, 2, BLK, D), BF16),
             vmem((3, NZ, PACK, 128), BF16),
             vmem((3, NZ - 1, PACK, 128), BF16),
             vmem((3, NZ, PACK, 128), BF16),
@@ -333,11 +363,13 @@
             vmem((2, 2, NX * TOK, NY * BLK), F32),
             vmem((2, NX, TOK, NY * BLK), BF16),
             vmem((2, NX - 1, TOK, D), BF16),
-            vmem((2, NX - 1, TOK, D), BF16),
+            vmem((2, 2, TOK, HALF), BF16),
+            vmem((2, 2, TOK, HALF), BF16),
+            vmem((2, 2, TOK, D), BF16),
             vmem((TOK, D), F32),
             dma((5,)), dma, dma((3,)), dma, dma((3,)), dma, dma((3, 2)), dma((NX, 2)), dma, dma((2,)),
-            dma, dma((3,)), dma, dma((3,)), dma, dma((3,)), dma, dma((3,)), dma, dma((3,)),
-            dma, dma((2,)),
+            dma, dma((3, 2)), dma((3,)), dma, dma((3,)), dma, dma((3,)), dma, dma((3,)), dma, dma((3,)),
+            dma, dma((2, 2)), dma((2,)),
         ],
         compiler_params=pltpu.CompilerParams(
             collective_id=0, has_side_effects=True, vmem_limit_bytes=56 << 20

time: 69.7 us -> 72.9 us (1.046)
  Pallas kernels: 68 us -> 71.1 us
    pallas_call x1, Pallas kernels: 68 us -> 71.1 us  [body(): pl.pallas_call(kernel, name='ttt_layer', out_shape=jax.ShapeDtypeStruct((...]
where the time goes in v4:
time: 72.9 us; the launch traced here: 72.7 us
  Pallas kernels  71.1 us (98%)
  local copies, waits for them, and re-layouts  1.62 us (2%)
    pallas_call x1, Pallas kernels, body(): pl.pallas_call(kernel, name='ttt_layer', out_shape=jax.ShapeDtypeStruct((...  71.1 us
    unnamed x1, local copies, waits for them, and re-layouts  1.62 us

profile of v4, /device:TPU:1, one launch (start us, length us, event | category | flops | bytes accessed | tf_op | source)
XLA Modules:
  0.0 72.7 jit_solution(17873380225276433248)
XLA Ops:
  0.0 71.1 %ttt_layer.1 = bf16[128,768]{1,0:T(8,128)(2,1)} custom-call(bf16[128,768]{1,0:T(8,128)(2,1)} %key_hbm.1, bf16[128,768]{1,0:T(8,128)(2,1)} %val_hbm.1, bf16[128,768]{1,0:T(8,128)(2,1)} %qry_hbm.1, f32[1,128]{1,0:T(1,128)} %bitcast.1, bf16[3,6,768]{2,1,0:T(8,128)(2,1)} %w_hbm.1), custom_call_target="tpu_custom_call" | custom-call | tf_op jit(solution)/shard_map/ttt_layer/pallas_call | solution.py:335
  71.1 1.6 %copy.7 = bf16[128,768]{1,0:T(8,128)(2,1)} copy(bf16[128,768]{1,0:T(8,128)(2,1)} %ttt_layer.1) | data formatting | bytes 393216

commit v5 on v4

--- a/solution.py
+++ b/solution.py
@@ -131,8 +131,8 @@
     send_tok(0, slot, r_tok.at[2, 0], xs[3])
     for kind in range(2):
         send_tok(kind, slot, r_tokc.at[0, kind], other)
-    for k in (2, 1, 3):
-        send(qn.at[1, y], qn.at[1, y], s_q, r_q.at[1], ys[k])
+    for k in (1, 3):
+        send(qn.at[1, y], qn.at[1, y], s_q, r_q.at[1, k - 1], ys[k])
     for m in (1, 2):
         for k in far_first_z:
             send(az0.at[m, z], az0.at[m, z], s_az0, r_az0.at[m], zs[k])
@@ -209,7 +209,7 @@
     tokens_in(2, 0, None)
     tokens_in(2, 1, None)
     for k in (2, 1, 3):
-        send(qn.at[0, x], qn.at[0, x], s_q, r_q.at[0], xs[k])
+        send(qn.at[0, x], qn.at[0, x], s_q, r_q.at[0, k - 1], xs[k])
     forward(2)
     for k in (0, 1, 3, 2):
         wait(ks.at[1, 0], r_tokc.at[k, 1])
@@ -225,19 +225,24 @@
             s_ry, r_ryv.at[m], r_ry.at[m], ys[1], ys[3],
         )
 
-    gradient(2)
     wait(w.at[2, pl.ds(0, NY - 1)], r_wy.at[2])
     for k in (0, 1, 3, 2):
         backward(k)
-    gradient(0)
-    gradient(1)
-
-    order = (2, 0, 1)
+    order = (0, 1, 2)
+    for m in order:
+        gradient(m)
     for m in order:
         hand_on(
             rys.at[m, (y + 1) % NY], rys.at[m, (y + 3) % NY], ryv.at[m], rym.at[m], ryr.at[m],
             s_ry, r_ryv.at[m], r_ry.at[m], ys[1], ys[3],
         )
+
+    above, below = (y + NY - 1) % NY, (y + 1) % NY
+    wait(qn.at[1, above], r_q.at[1, 0])
+    send(qn.at[1, above, :, first], qn.at[1, above, :, first], s_q, r_q.at[1, 1], ys[1])
+    wait(qn.at[1, below], r_q.at[1, 2])
+    send(qn.at[1, below, :, second], qn.at[1, below, :, second], s_q, r_q.at[1, 1], ys[3])
+
     unp[:, :, BLK:, :] = jnp.zeros((3, 6, 8, 128), F32)
     for m in order:
         wait(ryr.at[m], r_ry.at[m])
@@ -289,8 +294,9 @@
         )
         att[...] += dot_nn(hid_q[half, pos[1 - half]], down)
 
-    for axis in range(2):
-        wait(qn.at[axis, pl.ds(0, NX - 1)], r_q.at[axis])
+    for k in range(NX - 1):
+        wait(qn.at[0, 0], r_q.at[0, k])
+    wait(qn.at[1, 0], r_q.at[1, 1])
     for m in order:
         wait(wu.at[m, c, pl.ds(0, NY - 1)], r_ay.at[m])
         send(wu.at[m, c], wu.at[m, c], s_ac, r_ac.at[m], other)
@@ -367,12 +373,12 @@
             vmem((2, 2, TOK, HALF), BF16),
             vmem((2, 2, TOK, D), BF16),
             vmem((TOK, D), F32),
-            dma((5,)), dma, dma((3,)), dma, dma((3,)), dma, dma((3, 2)), dma((NX, 2)), dma, dma((2,)),
+            dma((5,)), dma, dma((3,)), dma, dma((3,)), dma, dma((3, 2)), dma((NX, 2)), dma, dma((2, 3)),
             dma, dma((3, 2)), dma((3,)), dma, dma((3,)), dma, dma((3,)), dma, dma((3,)), dma, dma((3,)),
             dma, dma((2, 2)), dma((2,)),
         ],
         compiler_params=pltpu.CompilerParams(
-            collective_id=0, has_side_effects=True, vmem_limit_bytes=56 << 20
+            collective_id=0, has_side_effects=True, vmem_limit_bytes=56250000
         ),
     )(key_tokens, value_tokens, queries, token_rate.reshape(1, TOK), fast_weights)
 

time: 72.9 us -> 68.7 us (0.942)
  Pallas kernels: 71.1 us -> 66.4 us
    pallas_call x1, Pallas kernels: 71.1 us -> 66.4 us  [body(): pl.pallas_call(kernel, name='ttt_layer', out_shape=jax.ShapeDtypeStruct((...]
    unnamed x1 -> x5, local copies, waits for them, and re-layouts: 1.62 us -> 2.1 us
where the time goes in v5:
time: 68.7 us; the launch traced here: 68.5 us
  Pallas kernels  66.4 us (97%)
  local copies, waits for them, and re-layouts  2.1 us (3%)
    pallas_call x1, Pallas kernels, body(): pl.pallas_call(kernel, name='ttt_layer', out_shape=jax.ShapeDtypeStruct((...  66.4 us
    unnamed x5, local copies, waits for them, and re-layouts  2.1 us

profile of v5, /device:TPU:1, one launch (start us, length us, event | category | flops | bytes accessed | tf_op | source)
XLA Modules:
  0.0 68.5 jit_solution(396574157417253707)
XLA Ops:
  0.0 0.0 copy-start.1
  0.0 0.7 copy-done.1
  0.7 0.0 copy-start
  0.7 0.8 %copy-done = bf16[3,6,768]{2,1,0:T(8,128)(2,1)S(1)} copy-done((bf16[3,6,768]{2,1,0:T(8,128)(2,1)S(1)}, bf16[3,6,768]{2,1,0:T(8,128)(2,1)}, u32[]{:S(2)}) %copy-start) | copy-done | bytes 27672
  1.4 66.4 %ttt_layer.1 = bf16[128,768]{1,0:T(8,128)(2,1)S(1)} custom-call(bf16[128,768]{1,0:T(8,128)(2,1)} %key_hbm.1, bf16[128,768]{1,0:T(8,128)(2,1)} %val_hbm.1, bf16[128,768]{1,0:T(8,128)(2,1)} %qry_hbm.1, f32[1,128]{1,0:T(1,128)S(1)} %bitcast.1, bf16[3,6,768]{2,1,0:T(8,128)(2,1)S(1)} %copy-done), custom_call_target="tpu_custom_call" | custom-call | tf_op jit(solution)/shard_map/ttt_layer/pallas_call | solution.py:341
  67.8 0.7 copy.7
Async XLA Ops:
  0.0 0.7 copy-start.1
  0.7 0.8 %copy-start = (bf16[3,6,768]{2,1,0:T(8,128)(2,1)S(1)}, bf16[3,6,768]{2,1,0:T(8,128)(2,1)}, u32[]{:S(2)}) copy-start(bf16[3,6,768]{2,1,0:T(8,128)(2,1)} %w_hbm.1) | copy-start | bytes 82948

commit v6 on v5

--- a/solution.py
+++ b/solution.py
@@ -58,7 +58,7 @@
     far_first_z = (4, 3, 5, 2, 6, 1, 7)
 
     barrier = pltpu.get_barrier_semaphore()
-    peers = [other] + xs[1:] + ys[1:] + zs[1:]
+    peers = [zs[k] for k in far_first_z] + [ys[2], xs[2], ys[1], ys[3], xs[1], xs[3], other]
     for peer in peers:
         pl.semaphore_signal(barrier, inc=1, device_id=peer, device_id_type=MESH)
 
@@ -191,26 +191,23 @@
         kn = chunk(0, k)
         gate = dot_nt(w[0].reshape(NY * BLK, D), kn)
         up = dot_nt(w[1].reshape(NY * BLK, D), kn)
-        gs[0, k] = gate
-        gs[1, k] = up
-        act[2, k] = (gate * jax.nn.sigmoid(gate) * up).astype(BF16)
+        sig = jax.nn.sigmoid(gate)
+        silu = gate * sig
+        act[2, k] = (silu * up).astype(BF16)
+        gs[0, k] = up * sig * (1.0 + gate * (1.0 - sig))
+        gs[1, k] = silu
 
     def backward(k):
         hgrad = dot_nt(w[2].reshape(NY * BLK, D), chunk(1, k))
-        gate, up = gs[0, k], gs[1, k]
-        sig = jax.nn.sigmoid(gate)
-        act[0, k] = (hgrad * up * sig * (1.0 + gate * (1.0 - sig))).astype(BF16)
-        act[1, k] = (hgrad * (gate * sig)).astype(BF16)
-
+        act[0, k] = (hgrad * gs[0, k]).astype(BF16)
+        act[1, k] = (hgrad * gs[1, k]).astype(BF16)
+
+    tokens_in(2, 0, None)
+    tokens_in(2, 1, None)
     wait(w.at[0, pl.ds(0, NY - 1)], r_wy.at[0])
     wait(w.at[1, pl.ds(0, NY - 1)], r_wy.at[1])
-    for k in (0, 1, 3):
+    for k in (0, 1, 3, 2):
         forward(k)
-    tokens_in(2, 0, None)
-    tokens_in(2, 1, None)
-    for k in (2, 1, 3):
-        send(qn.at[0, x], qn.at[0, x], s_q, r_q.at[0, k - 1], xs[k])
-    forward(2)
     for k in (0, 1, 3, 2):
         wait(ks.at[1, 0], r_tokc.at[k, 1])
 
@@ -254,6 +251,9 @@
             rzs[m, zz] = unp[m, :, zz * ROWS : zz * ROWS + 8, :].reshape(PACK, 128).astype(BF16)
         for k in far_first_z:
             send(rzs.at[m, (z + k) % NZ], rzr.at[m, k - 1], s_rz, r_rz.at[m], zs[k])
+
+    for k in (2, 1, 3):
+        send(qn.at[0, x], qn.at[0, x], s_q, r_q.at[0, k - 1], xs[k])
 
     for m in order:
         wait(rzr.at[m], r_rz.at[m])
@@ -298,15 +298,17 @@
         wait(qn.at[0, 0], r_q.at[0, k])
     wait(qn.at[1, 0], r_q.at[1, 1])
     for m in order:
+        if m == 2:
+            query_hidden(0)
+            wait(wu.at[0, 1 - c], r_ac.at[0])
+            project(0, 1, 1 - c)
         wait(wu.at[m, c, pl.ds(0, NY - 1)], r_ay.at[m])
         send(wu.at[m, c], wu.at[m, c], s_ac, r_ac.at[m], other)
         if m < 2:
             project(m, 0, c)
-    query_hidden(0)
     partial_outputs(0, c)
-    for m in (0, 1):
-        wait(wu.at[m, 1 - c], r_ac.at[m])
-        project(m, 1, 1 - c)
+    wait(wu.at[1, 1 - c], r_ac.at[1])
+    project(1, 1, 1 - c)
     query_hidden(1)
     wait(wu.at[2, 1 - c], r_ac.at[2])
     partial_outputs(1, 1 - c)

time: 68.7 us -> 67.7 us (0.985)
  Pallas kernels: 66.4 us -> 65.4 us
    pallas_call x1, Pallas kernels: 66.4 us -> 65.4 us  [body(): pl.pallas_call(kernel, name='ttt_layer', out_shape=jax.ShapeDtypeStruct((...]
where the time goes in v6:
time: 67.7 us; the launch traced here: 67.5 us
  Pallas kernels  65.4 us (97%)
  local copies, waits for them, and re-layouts  2.1 us (3%)
    pallas_call x1, Pallas kernels, body(): pl.pallas_call(kernel, name='ttt_layer', out_shape=jax.ShapeDtypeStruct((...  65.4 us
    unnamed x5, local copies, waits for them, and re-layouts  2.1 us

profile of v6, /device:TPU:1, one launch (start us, length us, event | category | flops | bytes accessed | tf_op | source)
XLA Modules:
  0.0 67.5 jit_solution(5983190607895302108)
XLA Ops:
  0.0 0.0 copy-start.1
  0.0 0.7 copy-done.1
  0.7 0.0 copy-start
  0.7 0.8 %copy-done = bf16[3,6,768]{2,1,0:T(8,128)(2,1)S(1)} copy-done((bf16[3,6,768]{2,1,0:T(8,128)(2,1)S(1)}, bf16[3,6,768]{2,1,0:T(8,128)(2,1)}, u32[]{:S(2)}) %copy-start) | copy-done | bytes 27672
  1.4 65.4 %ttt_layer.1 = bf16[128,768]{1,0:T(8,128)(2,1)S(1)} custom-call(bf16[128,768]{1,0:T(8,128)(2,1)} %key_hbm.1, bf16[128,768]{1,0:T(8,128)(2,1)} %val_hbm.1, bf16[128,768]{1,0:T(8,128)(2,1)} %qry_hbm.1, f32[1,128]{1,0:T(1,128)S(1)} %bitcast.1, bf16[3,6,768]{2,1,0:T(8,128)(2,1)S(1)} %copy-done), custom_call_target="tpu_custom_call" | custom-call | tf_op jit(solution)/shard_map/ttt_layer/pallas_call | solution.py:343
  66.9 0.7 %copy.7 = bf16[128,768]{1,0:T(8,128)(2,1)} copy(bf16[128,768]{1,0:T(8,128)(2,1)S(1)} %ttt_layer.1) | data formatting | bytes 393216
Async XLA Ops:
  0.0 0.7 copy-start.1
  0.7 0.8 %copy-start = (bf16[3,6,768]{2,1,0:T(8,128)(2,1)S(1)}, bf16[3,6,768]{2,1,0:T(8,128)(2,1)}, u32[]{:S(2)}) copy-start(bf16[3,6,768]{2,1,0:T(8,128)(2,1)} %w_hbm.1) | copy-start | bytes 82948

commit v7 on v6

--- a/solution.py
+++ b/solution.py
@@ -380,7 +380,7 @@
             dma, dma((2, 2)), dma((2,)),
         ],
         compiler_params=pltpu.CompilerParams(
-            collective_id=0, has_side_effects=True, vmem_limit_bytes=56250000
+            collective_id=0, has_side_effects=True, vmem_limit_bytes=56 << 20
         ),
     )(key_tokens, value_tokens, queries, token_rate.reshape(1, TOK), fast_weights)
 

time: 67.7 us -> 67.8 us (level)
  Pallas kernels: 65.4 us -> 66.1 us
    unnamed x5 -> x1, local copies, waits for them, and re-layouts: 2.1 us -> 1.62 us
where the time goes in v7:
time: 67.8 us; the launch traced here: 67.7 us
  Pallas kernels  66.1 us (97%)
  local copies, waits for them, and re-layouts  1.62 us (2%)
    pallas_call x1, Pallas kernels, body(): pl.pallas_call(kernel, name='ttt_layer', out_shape=jax.ShapeDtypeStruct((...  66.1 us
    unnamed x1, local copies, waits for them, and re-layouts  1.62 us

profile of v7, /device:TPU:1, one launch (start us, length us, event | category | flops | bytes accessed | tf_op | source)
XLA Modules:
  0.0 67.7 jit_solution(7474213387448434594)
XLA Ops:
  0.0 66.1 %ttt_layer.1 = bf16[128,768]{1,0:T(8,128)(2,1)} custom-call(bf16[128,768]{1,0:T(8,128)(2,1)} %key_hbm.1, bf16[128,768]{1,0:T(8,128)(2,1)} %val_hbm.1, bf16[128,768]{1,0:T(8,128)(2,1)} %qry_hbm.1, f32[1,128]{1,0:T(1,128)} %bitcast.1, bf16[3,6,768]{2,1,0:T(8,128)(2,1)} %w_hbm.1), custom_call_target="tpu_custom_call" | custom-call | tf_op jit(solution)/shard_map/ttt_layer/pallas_call | solution.py:343
  66.1 1.6 %copy.7 = bf16[128,768]{1,0:T(8,128)(2,1)} copy(bf16[128,768]{1,0:T(8,128)(2,1)} %ttt_layer.1) | data formatting | bytes 393216

commit v8 on v7

--- a/solution.py
+++ b/solution.py
@@ -39,9 +39,9 @@
 def kernel(
     key_hbm, val_hbm, qry_hbm, rate_hbm, w_hbm, out_ref,
     key_ref, val_ref, qry_ref, rate_ref, w_ref,
-    wpk, az0, w, ks, qn, gs, act, rys, ryv, rym, ryr, rzs, rzr, az1, wu, unp, gu, hid_q, ps, pv, pm, pr, att,
+    wpk, az0, w, ks, qn, gs, act, rys, ryv, rym, ryr, rzs, rzr, az1, wu, unp, gu, hid_q, ps, pv, pm, pr, att, held,
     s_in, s_az0, r_az0, s_wy, r_wy, s_tok, r_tok, r_tokc, s_q, r_q,
-    s_ry, r_ryv, r_ry, s_rz, r_rz, s_az, r_az, s_ay, r_ay, s_ac, r_ac, s_p, r_pv, r_p,
+    s_ry, r_ryv, r_ry, s_rz, r_rz, s_az, r_az, s_ay, r_ay, s_ac, r_ac, s_p, r_pv, r_p, s_out,
 ):
     g = lax.axis_index("grp")
     d = lax.axis_index("dev")
@@ -330,11 +330,20 @@
     wait(wu.at[:, 0], s_ac)
     wait(ps, s_p)
 
-    result = att[...]
     for half in range(2):
         wait(pr.at[half], r_p.at[half])
-        result = result + pr[half, 0].astype(F32) + pr[half, 1].astype(F32)
-    out_ref[...] = result.astype(BF16)
+    writes = []
+    for i in range(2):
+        rows = slice(i * 64, (i + 1) * 64)
+        result = att[rows, :]
+        for half in range(2):
+            result = result + pr[half, 0, rows, :].astype(F32) + pr[half, 1, rows, :].astype(F32)
+        held[rows, :] = result.astype(BF16)
+        part = pl.ds(i * 64, 64)
+        writes.append(pltpu.make_async_copy(held.at[part], out_ref.at[part], s_out.at[i]))
+        writes[i].start()
+    for write in writes:
+        write.wait()
 
 
 def body(key_tokens, value_tokens, queries, token_rate, fast_weights):
@@ -345,7 +354,7 @@
         name="ttt_layer",
         out_shape=jax.ShapeDtypeStruct((TOK, D), BF16),
         in_specs=[pl.BlockSpec(memory_space=pl.ANY)] * 5,
-        out_specs=pl.BlockSpec(memory_space=pltpu.VMEM),
+        out_specs=pl.BlockSpec(memory_space=pl.ANY),
         scratch_shapes=[
             vmem((TOK, D), BF16),
             vmem((TOK, D), BF16),
@@ -375,9 +384,10 @@
             vmem((2, 2, TOK, HALF), BF16),
             vmem((2, 2, TOK, D), BF16),
             vmem((TOK, D), F32),
+            vmem((TOK, D), BF16),
             dma((5,)), dma, dma((3,)), dma, dma((3,)), dma, dma((3, 2)), dma((NX, 2)), dma, dma((2, 3)),
             dma, dma((3, 2)), dma((3,)), dma, dma((3,)), dma, dma((3,)), dma, dma((3,)), dma, dma((3,)),
-            dma, dma((2, 2)), dma((2,)),
+            dma, dma((2, 2)), dma((2,)), dma((2,)),
         ],
         compiler_params=pltpu.CompilerParams(
             collective_id=0, has_side_effects=True, vmem_limit_bytes=56 << 20

time: 67.8 us -> 67.8 us (level)
  no operation moved by 1% of the time
where the time goes in v8:
time: 67.8 us; the launch traced here: 67.7 us
  Pallas kernels  66.1 us (97%)
  local copies, waits for them, and re-layouts  1.62 us (2%)
    pallas_call x1, Pallas kernels, body(): pl.pallas_call(kernel, name='ttt_layer', out_shape=jax.ShapeDtypeStruct((...  66.1 us
    unnamed x1, local copies, waits for them, and re-layouts  1.62 us

profile of v8, /device:TPU:1, one launch (start us, length us, event | category | flops | bytes accessed | tf_op | source)
XLA Modules:
  0.0 67.7 jit_solution(507897506468722768)
XLA Ops:
  0.0 66.1 %ttt_layer.1 = bf16[128,768]{1,0:T(8,128)(2,1)} custom-call(bf16[128,768]{1,0:T(8,128)(2,1)} %key_hbm.1, bf16[128,768]{1,0:T(8,128)(2,1)} %val_hbm.1, bf16[128,768]{1,0:T(8,128)(2,1)} %qry_hbm.1, f32[1,128]{1,0:T(1,128)} %bitcast.1, bf16[3,6,768]{2,1,0:T(8,128)(2,1)} %w_hbm.1), custom_call_target="tpu_custom_call" | custom-call | tf_op jit(solution)/shard_map/ttt_layer/pallas_call | solution.py:352
  66.1 1.6 %copy.7 = bf16[128,768]{1,0:T(8,128)(2,1)} copy(bf16[128,768]{1,0:T(8,128)(2,1)} %ttt_layer.1) | data formatting | bytes 393216
